TPU v7x, 32 devices: a whole 2x2x4 slice. The times are simulated.
32 devices in a mesh: groups: 2 (over x), row: 16 (over z, y, core).
Axes of the slice: x: 2, y: 2, z: 4, core: 2. Of those that a mesh axis runs over, the one named last changes fastest.
Arguments:
- tokens: bfloat16 [2048, 5120], P(('groups', 'row')), parts along dimension 0, may hold values from -6 to 6
- w_query: bfloat16 [5120, 2048], P(None, 'row'), may hold values from -0.078125 to 0.078125
- w_key: bfloat16 [5120, 256], P(None, 'row'), may hold values from -0.078125 to 0.078125
- w_value: bfloat16 [5120, 256], P(None, 'row'), may hold values from -0.078125 to 0.078125
- q_gain: float32 [16, 128], P('row'), may hold values from 0.1 to 1.9
- k_gain: float32 [2, 128], replicated, may hold values from 0.1 to 1.9
Outputs:
- attended: bfloat16 [2048, 2048], P('groups', 'row'), parts along dimension 0
There are 2 independent parts, one for each index of `groups`. A program takes and returns all parts, laid end to end along the dimension named above; an argument that names none is the same for every part. Nothing has to cross between parts.
All inputs are finite; a program needn't handle non-finite values.
Results may differ from a plain program's by a relative error of at most 0.0082.
Values may be sent and summed in bfloat16 or wider, within the bound.
A program may use at most 128 MiB of HBM per device.

v0:
```python
import jax
import jax.numpy as jnp
from jax import lax
from jax.sharding import PartitionSpec as P

GROUP = 8


EPS = 1e-06
THETA = 1000000.0


def swapped(block, axis, apart):
    count = lax.axis_size(axis)
    route = []
    for low in range(count):
        high = low | 1 << apart
        if high != low and high < count:
            route += [(low, high), (high, low)]
    return lax.ppermute(block, axis, route)


def rope_tables(count, width):
    half = width // 2
    freq = THETA ** (-(jnp.arange(half, dtype=jnp.float32) * 2.0 / width))
    angles = jnp.arange(count, dtype=jnp.float32)[:, None] * freq[None, :]
    cosine = jnp.cos(angles)
    sine = jnp.sin(angles)
    return (jnp.concatenate([cosine, cosine], 1), jnp.concatenate([sine, sine], 1))


def norm_rope(raw, gain, cosine, sine):
    values = raw.astype(jnp.float32)
    scale = lax.rsqrt(jnp.mean(values * values, -1, keepdims=True) + EPS)
    normed = values * scale * gain
    half = normed.shape[-1] // 2
    turned = jnp.concatenate([-normed[:, half:], normed[:, :half]], 1)
    return (normed * cosine + turned * sine).astype(jnp.bfloat16)


def attend(query, start, key, value):
    width = query.shape[1]
    scores = jnp.dot(query, key.T, preferred_element_type=jnp.float32) * float(width) ** (-0.5)
    rows = start + lax.broadcasted_iota(jnp.int32, scores.shape, 0)
    cols = lax.broadcasted_iota(jnp.int32, scores.shape, 1)
    scores = jnp.where(cols <= rows, scores, jnp.float32(-1e30))
    top = jnp.max(scores, -1, keepdims=True)
    weights = jnp.exp(scores - top)
    total = jnp.sum(weights, -1, keepdims=True)
    probs = (weights / total).astype(jnp.bfloat16)
    return jnp.dot(probs, value, preferred_element_type=jnp.float32).astype(jnp.bfloat16)


def order_pair(mine, other, upper):
    lower_part = jnp.where(upper, other, mine)
    upper_part = jnp.where(upper, mine, other)
    return jnp.concatenate([lower_part, upper_part], 1)


def per_device(tokens, w_query, w_key, w_value, q_gain, k_gain):
    devices = lax.axis_size("row")
    owner = lax.axis_index("row")
    head_size = w_query.shape[1]
    count = tokens.shape[0] * devices
    shared = owner // GROUP
    levels = GROUP.bit_length() - 1
    merged = jnp.concatenate([w_query, w_key, w_value], 1)
    projected = jnp.dot(
        lax.all_gather(tokens, "row", axis=0, tiled=True),
        merged,
        preferred_element_type=jnp.float32,
    ).astype(jnp.bfloat16)
    query = projected[:, :head_size]
    key_cols = w_key.shape[1]
    key = projected[:, head_size : head_size + key_cols]
    value = projected[:, head_size + key_cols :]
    for level in range(levels):
        k_other, v_other = swapped((key, value), "row", level)
        upper = owner >> level & 1 == 1
        key = order_pair(key, k_other, upper)
        value = order_pair(value, v_other, upper)
    cosine, sine = rope_tables(count, head_size)
    q_rot = norm_rope(query, q_gain, cosine, sine)
    k_rot = norm_rope(key, lax.dynamic_slice_in_dim(k_gain, shared, 1, 0), cosine, sine)
    block = min(512, count)
    outputs = []
    for index in range(count // block):
        start = index * block
        finish = start + block
        outputs.append(attend(q_rot[start:finish], start, k_rot[:finish], value[:finish]))
    return jnp.concatenate(outputs, 0)


def solution(mesh):
    in_specs = (
        P(("groups", "row"), None),
        P(None, "row"),
        P(None, "row"),
        P(None, "row"),
        P("row", None),
        P(),
    )
    out_specs = P("groups", "row")
    return jax.shard_map(
        per_device, mesh=mesh, in_specs=in_specs, out_specs=out_specs, check_vma=False
    )
```

profile of v0, /device:TPU:0, one launch (start us, length us, event | category | flops | bytes accessed | tf_op | source)
XLA Modules:
  0.0 133.5 jit_solution(196523848760730192)
XLA Ops:
  6.5 0.0 copy-start
  6.5 0.0 copy-start.1
  6.5 0.0 all-gather.2.cloned.1.call-start
  6.5 0.7 all-gather.2.cloned.1.call-update
  7.3 1.5 %copy.7 = bf16[5120,16]{1,0:T(8,128)(2,1)S(1)} copy(bf16[5120,16]{0,1:T(8,128)(2,1)} %param.8) | data formatting | bytes 327680 | tf_op args[2]
  8.8 0.0 copy-done.1
  8.8 0.6 copy.8
  9.4 0.0 copy-done
  9.4 1.0 fusion.29
  10.4 0.0 copy-start.2
  10.4 89.8 %all-gather.2.cloned.1.call-done = bf16[1024,5120]{1,0:T(8,128)(2,1)} async-done(((bf16[64,5120]{1,0:T(8,128)(2,1)}), bf16[1024,5120]{1,0:T(8,128)(2,1)}) %all-gather.2.cloned.1.call-update) | async-done | bytes 10485776 | tf_op jit(solution)/shard_map/all_gather | solution.py:69
  100.3 8.4 %fusion.11 = bf16[1024,160]{0,1:T(8,128)(2,1)S(1)} fusion(bf16[1024,5120]{1,0:T(8,128)(2,1)} %all-gather.2.cloned.1.call-done, bf16[5120,16]{1,0:T(8,128)(2,1)S(1)} %copy.8, bf16[5120,16]{1,0:T(8,128)(2,1)S(1)} %copy.7, bf16[5120,128]{1,0:T(8,128)(2,1)} %param.7), kind=kOutput, calls=%fused_computation.14 | convolution fusion | flops 1682800640 | bytes 12451840 | tf_op jit(solution)/shard_map/dot_general | solution.py:68
  108.7 0.1 fusion.15
  108.7 0.3 collective-permute-start.3
  109.1 0.0 copy-done.2
  109.1 0.1 fusion.16
  109.2 0.8 collective-permute-done.3
  110.0 0.3 collective-permute-start
  110.4 0.5 collective-permute-start.4
  110.9 0.4 collective-permute-done
  111.3 1.2 collective-permute-start.1
  112.5 2.5 %collective-permute-done.4 = bf16[1024,32]{0,1:T(8,128)(2,1)S(1)} collective-permute-done((bf16[1024,32]{0,1:T(8,128)(2,1)S(1)}, bf16[1024,32]{0,1:T(8,128)(2,1)S(1)}, u32[]{:S(2)}, u32[]{:S(2)}) %collective-permute-start.4) | collective-permute-done | bytes 65568 | tf_op jit(solution)/shard_map/ppermute | solution.py:20
  115.0 0.6 collective-permute-start.5
  115.6 0.4 collective-permute-done.1
  116.1 1.2 collective-permute-start.2
  117.2 4.0 %collective-permute-done.5 = bf16[1024,64]{0,1:T(8,128)(2,1)S(1)} collective-permute-done((bf16[1024,64]{0,1:T(8,128)(2,1)S(1)}, bf16[1024,64]{0,1:T(8,128)(2,1)S(1)}, u32[]{:S(2)}, u32[]{:S(2)}) %collective-permute-start.5) | collective-permute-done | bytes 131104 | tf_op jit(solution)/shard_map/ppermute | solution.py:20
  121.3 1.4 %collective-permute-done.2 = bf16[1024,64]{0,1:T(8,128)(2,1)S(1)} collective-permute-done((bf16[1024,64]{0,1:T(8,128)(2,1)S(1)}, bf16[1024,64]{0,1:T(8,128)(2,1)S(1)}, u32[]{:S(2)}, u32[]{:S(2)}) %collective-permute-start.2) | collective-permute-done | bytes 131104 | tf_op jit(solution)/shard_map/ppermute | solution.py:20
  122.7 0.1 fusion.17
  122.8 0.1 fusion.18
  123.0 0.3 fusion.22
  123.3 0.4 fusion.41
  123.6 0.6 fusion.40
  124.3 0.2 fusion.14
  124.5 0.5 fusion.6
  125.0 0.4 convolution_convert_fusion
  125.4 0.5 convolution_convert_fusion.1
  125.9 0.7 pad_maximum_fusion.3
  (18 shorter events, 0.3 us)
Async XLA Ops:
  6.5 2.9 %copy-start = (f32[2,128]{1,0:T(2,128)S(1)}, f32[2,128]{1,0:T(2,128)}, u32[]{:S(2)}) copy-start(f32[2,128]{1,0:T(2,128)} %param.11) | copy-start | bytes 3076
  6.5 2.2 %copy-start.1 = (bf16[5120,16]{0,1:T(8,128)(2,1)S(1)}, bf16[5120,16]{0,1:T(8,128)(2,1)}, u32[]{:S(2)}) copy-start(bf16[5120,16]{0,1:T(8,128)(2,1)} %param.9) | copy-start | bytes 491524
  6.5 93.7 %all-gather.2.cloned.1.call-start = ((), (), s32[]{:S(2)}) async-start(), calls=%async_computation | async-start | bytes 11141120 | tf_op jit(solution)/shard_map/all_gather | solution.py:69
  10.4 98.6 %copy-start.2 = (f32[1,128]{1,0:T(1,128)S(1)}, f32[1,128]{1,0:T(1,128)}, u32[]{:S(2)}) copy-start(f32[1,128]{1,0:T(1,128)} %param.10) | copy-start | bytes 1540
  108.7 1.3 collective-permute-start.3
  110.0 1.3 collective-permute-start
  110.4 4.6 %collective-permute-start.4 = (bf16[1024,32]{0,1:T(8,128)(2,1)S(1)}, bf16[1024,32]{0,1:T(8,128)(2,1)S(1)}, u32[]{:S(2)}, u32[]{:S(2)}) collective-permute-start(bf16[1024,32]{0,1:T(8,128)(2,1)S(1)} %pad_maximum_fusion.7), channel_id=1, source_target_pairs={{0,2},{2,0},{1,3},{3,1},{4,6},{6,4},{5,7},{7,5},{8,10},{10,8},{9,1... | collective-permute-start | bytes 196616 | tf_op jit(solution)/shard_map/ppermute | solution.py:20
  111.3 4.7 %collective-permute-start.1 = (bf16[1024,32]{0,1:T(8,128)(2,1)S(1)}, bf16[1024,32]{0,1:T(8,128)(2,1)S(1)}, u32[]{:S(2)}, u32[]{:S(2)}) collective-permute-start(bf16[1024,32]{0,1:T(8,128)(2,1)S(1)} %pad_maximum_fusion.6), channel_id=1, source_target_pairs={{0,2},{2,0},{1,3},{3,1},{4,6},{6,4},{5,7},{7,5},{8,10},{10,8},{9,1... | collective-permute-start | bytes 196616 | tf_op jit(solution)/shard_map/ppermute | solution.py:20
  115.0 6.2 %collective-permute-start.5 = (bf16[1024,64]{0,1:T(8,128)(2,1)S(1)}, bf16[1024,64]{0,1:T(8,128)(2,1)S(1)}, u32[]{:S(2)}, u32[]{:S(2)}) collective-permute-start(bf16[1024,64]{0,1:T(8,128)(2,1)S(1)} %pad_maximum_fusion.5), channel_id=1, source_target_pairs={{0,4},{4,0},{1,5},{5,1},{2,6},{6,2},{3,7},{7,3},{8,12},{12,8},{9,1... | collective-permute-start | bytes 393224 | tf_op jit(solution)/shard_map/ppermute | solution.py:20
  116.1 6.6 %collective-permute-start.2 = (bf16[1024,64]{0,1:T(8,128)(2,1)S(1)}, bf16[1024,64]{0,1:T(8,128)(2,1)S(1)}, u32[]{:S(2)}, u32[]{:S(2)}) collective-permute-start(bf16[1024,64]{0,1:T(8,128)(2,1)S(1)} %pad_maximum_fusion.4), channel_id=1, source_target_pairs={{0,4},{4,0},{1,5},{5,1},{2,6},{6,2},{3,7},{7,3},{8,12},{12,8},{9,1... | collective-permute-start | bytes 393224 | tf_op jit(solution)/shard_map/ppermute | solution.py:20
Sparse Core Ops, SparseCore 0:
  9.6 90.5 all-gather.1
where the time goes:
time: 134 us; the launch traced here: 133 us
  waiting for transfers between devices  100 us (75%)
  between operations  13.6 us (10%)
  matrix products  10.3 us (8%)
  starting transfers between devices  4.1 us (3%)
  other arithmetic  3.37 us (3%)
  local copies, waits for them, and re-layouts  2.09 us (2%)
    all_gather x1, waiting for transfers between devices, per_device(): lax.all_gather(tokens, 'row', axis=0, tiled=True)  89.8 us
    ppermute x6, waiting for transfers between devices, swapped(): return lax.ppermute(block, axis, route)  9.48 us
    dot_general x1, matrix products, per_device(): jnp.dot(lax.all_gather(tokens, 'row', axis=0, tiled=True), merged, prefer...  8.38 us
    ppermute x6, starting transfers between devices, swapped(): return lax.ppermute(block, axis, route)  4.1 us
  transfers between devices with their start and end apart: 7, of which 7 were waited for; matrix products, arithmetic and copies ran while one was open for 3% of the time, Pallas kernels for 0%

commit v1 on v0

--- a/solution.py
+++ b/solution.py
@@ -1,6 +1,8 @@
 import jax
 import jax.numpy as jnp
 from jax import lax
+from jax.experimental import pallas as pl
+from jax.experimental.pallas import tpu as pltpu
 from jax.sharding import PartitionSpec as P
 
 GROUP = 8
@@ -57,7 +59,7 @@
     return jnp.concatenate([lower_part, upper_part], 1)
 
 
-def per_device(tokens, w_query, w_key, w_value, q_gain, k_gain):
+def gathered_device(tokens, w_query, w_key, w_value, q_gain, k_gain):
     devices = lax.axis_size("row")
     owner = lax.axis_index("row")
     head_size = w_query.shape[1]
@@ -91,6 +93,388 @@
     return jnp.concatenate(outputs, 0)
 
 
+LINE, PLANE = 4, 4
+CHUNKS = 4
+PARTS = 8
+
+
+def layer_kernel(
+    tokens, w_query, w_kv_k, w_kv_v, q_gain, k_gain, freq, out,
+    tok, wq, wkv, q_stage, q_all, kv_all, cos_t, sin_t, acc_q, acc_kv,
+    local_sem, right_send, left_send, tok_recv,
+    core_send, core_recv, y_send, x_send, w_recv, diag_send, diag_recv,
+    q_send, q_recv, kv_send, kv_recv,
+):
+    me = lax.axis_index("row")
+    g = lax.axis_index("groups")
+    z, s = me // PLANE, me % PLANE
+    y, c = s // 2, s % 2
+    peers = [s, y * 2 + 1 - c, (1 - y) * 2 + c, (1 - y) * 2 + 1 - c]
+    half = z % 2
+    pair_z = z + 1 - 2 * half
+    shared = z // 2
+    rows, width = tokens.shape
+    head = w_query.shape[1]
+    step = width // CHUNKS
+    part = width // PARTS
+
+    def at(zz, ss):
+        return {"row": zz * PLANE + ss}
+
+    barrier = pltpu.get_barrier_semaphore()
+    friends = [at(z, p) for p in peers[1:]] + [at(pair_z, p) for p in peers]
+    friends.append({"groups": 1 - g})
+    for friend in friends:
+        pl.semaphore_signal(barrier, inc=1, device_id=friend)
+    far_z = z - 1 + 2 * half
+    has_far = jnp.logical_and(far_z >= 0, far_z < LINE)
+
+    @pl.when(has_far)
+    def _():
+        pl.semaphore_signal(barrier, inc=1, device_id=at(far_z, s))
+
+    def own(src, dst, index):
+        return pltpu.make_async_copy(src, dst, local_sem.at[index])
+
+    locals_ = [
+        own(w_kv_k, wkv.at[0, s], 0),
+        own(w_kv_v, wkv.at[1, s], 1),
+        own(tokens, tok.at[z], 2),
+        own(w_query, wq.at[:, pl.ds(0, head)], 3),
+    ]
+    for copy in locals_:
+        copy.start()
+
+    pl.semaphore_wait(barrier, len(friends) + jnp.where(has_far, 1, 0))
+
+    def remote(src, dst, send, recv, device):
+        return pltpu.make_async_remote_copy(src, dst, send, recv, device_id=device)
+
+    def token_copy(block, chunk, right, src=None):
+        view = tok.at[block, :, pl.ds(chunk * step, step)]
+        sems = right_send if right else left_send
+        return remote(
+            view if src is None else src, view, sems.at[block, chunk],
+            tok_recv.at[block, chunk], at(z + 1 if right else z - 1, s),
+        )
+
+    for chunk in range(CHUNKS):
+        view = tokens.at[:, pl.ds(chunk * step, step)]
+
+        @pl.when(z > 0)
+        def _():
+            token_copy(z, chunk, False, view).start()
+
+        @pl.when(z < LINE - 1)
+        def _():
+            token_copy(z, chunk, True, view).start()
+
+    last_piece = PARTS // 2
+
+    def piece(i, parity, slot):
+        if i == last_piece:
+            return wkv.at[parity, peers[slot]], PARTS + parity
+        index = 2 * i + parity
+        rows_ = pl.ds(pl.multiple_of(index * part, part), part)
+        return wq.at[rows_, pl.ds(slot * head, head)], index
+
+    def y_copy(i):
+        view, index = piece(i, g, 2)
+        mine, _ = piece(i, g, 0)
+        if i == last_piece:
+            view = mine
+        return remote(mine, view, y_send.at[i], w_recv.at[index], at(z, peers[2]))
+
+    def y_arrival(i):
+        view, index = piece(i, g, 2)
+        return remote(view, view, y_send.at[i], w_recv.at[index], at(z, peers[2]))
+
+    def x_copy(i, parity):
+        view, index = piece(i, parity, 2)
+        return remote(view, view, x_send.at[i], w_recv.at[index], {"groups": 1 - g})
+
+    def diag_copy(i, parity):
+        view, index = piece(i, parity, 2)
+        if i == last_piece:
+            there = view
+        else:
+            there, _ = piece(i, parity, 3)
+        return remote(view, there, diag_send.at[index], diag_recv.at[index], at(z, peers[1]))
+
+    def diag_arrival(i, parity):
+        view, index = piece(i, parity, 3)
+        return remote(view, view, diag_send.at[index], diag_recv.at[index], at(z, peers[1]))
+
+    def core_copies(incoming):
+        whose = peers[1] if incoming else s
+        cols = pl.ds(head, head)
+        mine = wq.at[:, cols] if incoming else wq.at[:, pl.ds(0, head)]
+        return [
+            remote(wkv.at[i, whose], wkv.at[i, whose], core_send.at[i], core_recv.at[i], at(z, peers[1]))
+            for i in (0, 1)
+        ] + [remote(mine, wq.at[:, cols], core_send.at[2], core_recv.at[2], at(z, peers[1]))]
+
+    for copy in locals_:
+        copy.wait()
+    for i in range(last_piece + 1):
+        y_copy(i).start()
+    for copy in core_copies(False):
+        copy.start()
+
+    spot = lax.broadcasted_iota(jnp.int32, cos_t.shape, 0).astype(jnp.float32)
+    angle = spot * freq[...]
+    lane = lax.broadcasted_iota(jnp.int32, cos_t.shape, 1)
+    cos_t[...] = jnp.cos(angle)
+    sine = jnp.sin(angle)
+    sin_t[...] = jnp.where(lane < head // 2, -sine, sine)
+
+    def pass_on(distance, chunk):
+        low, high = z - distance, z + distance
+
+        @pl.when(low >= 0)
+        def _():
+            token_copy(low, chunk, True).wait_recv()
+
+            @pl.when(z < LINE - 1)
+            def _():
+                token_copy(low, chunk, True).start()
+
+        @pl.when(high < LINE)
+        def _():
+            token_copy(high, chunk, False).wait_recv()
+
+            @pl.when(z > 0)
+            def _():
+                token_copy(high, chunk, False).start()
+
+    def take_x(i):
+        x_copy(i, 1 - g).wait_recv()
+        diag_copy(i, 1 - g).start()
+
+    for i in range(last_piece + 1):
+        y_arrival(i).wait_recv()
+        x_copy(i, g).start()
+        diag_copy(i, g).start()
+        if i < CHUNKS:
+            pass_on(1, i)
+        if i > 0:
+            take_x(i - 1)
+    take_x(last_piece)
+    for copy in core_copies(True):
+        copy.wait_recv()
+    for i in range(last_piece + 1):
+        diag_arrival(i, g).wait_recv()
+        diag_arrival(i, 1 - g).wait_recv()
+
+    def result_copies(block):
+        place = block * PLANE + s
+        copies = []
+        for t in (1, 2, 3):
+            copies.append(remote(
+                q_stage.at[block, t - 1], q_all.at[place], q_send.at[block, t - 1],
+                q_recv.at[block, t - 1], at(z, peers[t]),
+            ))
+        for far in (0, 1):
+            for t in range(PLANE):
+                if far == 0 and t == 0:
+                    continue
+                i = far * PLANE + t - 1
+                copies.append(remote(
+                    kv_all.at[half, place], kv_all.at[half, place], kv_send.at[block, i],
+                    kv_recv.at[block, i], at(pair_z if far else z, peers[t]),
+                ))
+        return copies
+
+    def result_arrivals(block):
+        arrivals = []
+        for t in (1, 2, 3):
+            place = q_all.at[block * PLANE + peers[t]]
+            arrivals.append(remote(
+                place, place, q_send.at[block, t - 1], q_recv.at[block, t - 1], at(z, peers[t]),
+            ))
+        for far in (0, 1):
+            for t in range(PLANE):
+                if far == 0 and t == 0:
+                    continue
+                i = far * PLANE + t - 1
+                place = kv_all.at[1 - half if far else half, block * PLANE + peers[t]]
+                arrivals.append(remote(
+                    place, place, kv_send.at[block, i], kv_recv.at[block, i],
+                    at(pair_z if far else z, peers[t]),
+                ))
+        return arrivals
+
+    def finish(block, q_sum, kv_sum):
+        q_bf = q_sum.astype(jnp.bfloat16)
+        place = block * PLANE + s
+        q_all[place] = q_bf[:, :head]
+        for t in (1, 2, 3):
+            q_stage[block, t - 1] = q_bf[:, t * head : (t + 1) * head]
+        kv_all[half, place] = kv_sum.astype(jnp.bfloat16)
+        for copy in result_copies(block):
+            copy.start()
+
+    def products(block, cols):
+        part_tok = tok[block, :, cols]
+        q_part = jnp.dot(part_tok, wq[cols, :], preferred_element_type=jnp.float32)
+        kv_w = wkv[:, :, :, cols]
+        kv_w = kv_w.reshape(kv_w.shape[0] * kv_w.shape[1] * kv_w.shape[2], kv_w.shape[3])
+        kv_part = lax.dot_general(
+            part_tok, kv_w, (((1,), (1,)), ((), ())), preferred_element_type=jnp.float32
+        )
+        return q_part, kv_part
+
+    def project(block, before):
+        acc_q[...] = jnp.zeros_like(acc_q)
+        acc_kv[...] = jnp.zeros_like(acc_kv)
+        for chunk in range(CHUNKS):
+            before(chunk)
+            q_part, kv_part = products(block, pl.ds(chunk * step, step))
+            acc_q[...] += q_part
+            acc_kv[...] += kv_part
+        finish(block, acc_q[...], acc_kv[...])
+
+    project(z, lambda chunk: None)
+    for chunk in range(CHUNKS):
+        pass_on(2, chunk)
+    for distance in (1, 2):
+
+        @pl.loop(0, 2)
+        def _(side):
+            block = z - distance + 2 * distance * side
+
+            @pl.when(jnp.logical_and(block >= 0, block < LINE))
+            def _():
+                project(block, lambda chunk: None)
+
+    @pl.when(jnp.logical_or(z == 0, z == LINE - 1))
+    def _():
+        project(LINE - 1 - z, lambda chunk: pass_on(3, chunk))
+
+    @pl.loop(0, LINE)
+    def _(block):
+        for copy in result_arrivals(block):
+            copy.wait_recv()
+
+    count = rows * PLANE * LINE
+    low_half = lax.broadcasted_iota(jnp.int32, (count, head), 1) < head // 2
+    kv_0 = kv_all[0].reshape(count, head).astype(jnp.float32)
+    kv_1 = kv_all[1].reshape(count, head).astype(jnp.float32)
+    key = jnp.where(low_half, kv_0, pltpu.roll(kv_1, head // 2, 1))
+    value = jnp.where(low_half, pltpu.roll(kv_0, head // 2, 1), kv_1).astype(jnp.bfloat16)
+    value = jnp.concatenate([value, jnp.ones_like(value)], 1)
+
+    def turn(values, gain, where):
+        scale = lax.rsqrt(jnp.mean(values * values, -1, keepdims=True) + EPS)
+        normed = values * scale * gain
+        return (normed * cos_t[where] + pltpu.roll(normed, head // 2, 1) * sin_t[where]).astype(jnp.bfloat16)
+
+    everything = slice(0, count)
+    query = q_all[...].reshape(count, head).astype(jnp.float32)
+    q_rot = turn(query, q_gain[...], everything)
+    k_rot = turn(key, k_gain[pl.ds(shared, 1), :], everything)
+    tile = rows * PLANE
+    factor = float(head) ** (-0.5) * 1.4426950408889634
+    for i in range(LINE):
+        scores = lax.dot_general(
+            q_rot[i * tile : (i + 1) * tile], k_rot[: (i + 1) * tile], (((1,), (1,)), ((), ())),
+            preferred_element_type=jnp.float32,
+        )
+        weights = jnp.exp2(scores * factor)
+        at_row = i * tile + lax.broadcasted_iota(jnp.int32, scores.shape, 0)
+        at_col = lax.broadcasted_iota(jnp.int32, scores.shape, 1)
+        weights = jnp.where(at_col <= at_row, weights, 0.0).astype(jnp.bfloat16)
+        total = jnp.dot(weights, value[: (i + 1) * tile], preferred_element_type=jnp.float32)
+        out[i * tile : (i + 1) * tile, :] = (total[:, :head] / total[:, head:]).astype(out.dtype)
+
+    for chunk in range(CHUNKS):
+        for block in range(LINE):
+
+            @pl.when(jnp.logical_and(block <= z, z < LINE - 1))
+            def _():
+                token_copy(block, chunk, True).wait_send()
+
+            @pl.when(jnp.logical_and(block >= z, z > 0))
+            def _():
+                token_copy(block, chunk, False).wait_send()
+
+    for i in range(last_piece + 1):
+        y_copy(i).wait_send()
+        x_copy(i, g).wait_send()
+        diag_copy(i, g).wait_send()
+        diag_copy(i, 1 - g).wait_send()
+    for copy in core_copies(False):
+        copy.wait_send()
+
+    @pl.loop(0, LINE)
+    def _(block):
+        for copy in result_copies(block):
+            copy.wait_send()
+
+
+def kernel_device(tokens, w_query, w_key, w_value, q_gain, k_gain):
+    rows, width = tokens.shape
+    head = w_query.shape[1]
+    thin = w_key.shape[1]
+    count = rows * lax.axis_size("row")
+    half = head // 2
+    freq = THETA ** (-(jnp.arange(half, dtype=jnp.float32) * 2.0 / head))
+    freq = jnp.concatenate([freq, freq])[None, :]
+    bf16, f32 = jnp.bfloat16, jnp.float32
+    dma = pltpu.SemaphoreType.DMA
+    hbm = pl.BlockSpec(memory_space=pl.ANY)
+    vmem = pl.BlockSpec(memory_space=pltpu.VMEM)
+    blocks = LINE * PLANE
+    return pl.pallas_call(
+        layer_kernel,
+        out_shape=jax.ShapeDtypeStruct((count, head), bf16),
+        in_specs=[hbm] * 4 + [vmem] * 3,
+        out_specs=vmem,
+        scratch_shapes=[
+            pltpu.VMEM((LINE, rows, width), bf16),
+            pltpu.VMEM((width, PLANE * head), bf16),
+            pltpu.VMEM((2, PLANE, thin, width), bf16),
+            pltpu.VMEM((LINE, PLANE - 1, rows, head), bf16),
+            pltpu.VMEM((blocks, rows, head), bf16),
+            pltpu.VMEM((2, blocks, rows, 2 * PLANE * thin), bf16),
+            pltpu.VMEM((count, head), f32),
+            pltpu.VMEM((count, head), f32),
+            pltpu.VMEM((rows, PLANE * head), f32),
+            pltpu.VMEM((rows, 2 * PLANE * thin), f32),
+            dma((4,)),
+            dma((LINE, CHUNKS)),
+            dma((LINE, CHUNKS)),
+            dma((LINE, CHUNKS)),
+            dma((3,)),
+            dma((3,)),
+            dma((PARTS // 2 + 1,)),
+            dma((PARTS // 2 + 1,)),
+            dma((PARTS + 2,)),
+            dma((PARTS + 2,)),
+            dma((PARTS + 2,)),
+            dma((LINE, 3)),
+            dma((LINE, 3)),
+            dma((LINE, 7)),
+            dma((LINE, 7)),
+        ],
+        compiler_params=pltpu.CompilerParams(
+            collective_id=0, has_side_effects=True, vmem_limit_bytes=48 * 1024 * 1024
+        ),
+    )(tokens, w_query, w_key.T, w_value.T, q_gain, k_gain, freq)
+
+
+def per_device(*args):
+    fits = (
+        lax.axis_size("row") == LINE * PLANE
+        and lax.axis_size("groups") == 2
+        and args[0].shape[0] <= 64
+        and args[0].shape[1] % (PARTS * 128) == 0
+        and args[1].shape[1] == 128
+        and args[2].shape[1] * GROUP == 128
+    )
+    return kernel_device(*args) if fits else gathered_device(*args)
+
+
 def solution(mesh):
     in_specs = (
         P(("groups", "row"), None),

time: 134 us -> 65.1 us (0.49)
  waiting for transfers between devices: 100 us -> 0 us
  Pallas kernels: 0 us -> 58.5 us
  between operations: 13.6 us -> 0.02 us
  matrix products: 10.3 us -> 0 us
  local copies, waits for them, and re-layouts: 2.09 us -> 6.28 us
  starting transfers between devices: 4.1 us -> 0 us
  other arithmetic: 3.37 us -> 0.09 us
    all_gather x1 -> x0, waiting for transfers between devices: 89.8 us -> none  [per_device(): lax.all_gather(tokens, 'row', axis=0, tiled=True)]
    pallas_call x0 -> x1, Pallas kernels: none -> 58.5 us  [kernel_device(): pl.pallas_call(layer_kernel, out_shape=jax.ShapeDtypeStruct((count, head)...]
    dot_general x5 -> x0, matrix products: 10.3 us -> none  [the longest x1 8.38 us: per_device(): jnp.dot(lax.all_gather(tokens, 'row', axis=0, tiled=True), merged, prefer...]
    ppermute x6 -> x0, waiting for transfers between devices: 9.48 us -> none  [swapped(): return lax.ppermute(block, axis, route)]
    unnamed x8 -> x13, local copies, waits for them, and re-layouts: 2.08 us -> 6.28 us
    ppermute x6 -> x0, starting transfers between devices: 4.1 us -> none  [swapped(): return lax.ppermute(block, axis, route)]
  transfers between devices with their start and end apart: 7 -> 0, of which waited for: 7 -> 0; matrix products, arithmetic and copies ran while one was open for 3% -> 0% of each run, Pallas kernels for 0% -> 0%
where the time goes in v1:
time: 65.1 us; the launch traced here: 64.9 us
  Pallas kernels  58.5 us (90%)
  local copies, waits for them, and re-layouts  6.28 us (10%)
    pallas_call x1, Pallas kernels, kernel_device(): pl.pallas_call(layer_kernel, out_shape=jax.ShapeDtypeStruct((count, head)...  58.5 us
    unnamed x13, local copies, waits for them, and re-layouts  6.28 us

profile of v1, /device:TPU:0, one launch (start us, length us, event | category | flops | bytes accessed | tf_op | source)
XLA Modules:
  0.0 64.9 jit_solution(7362870699665295078)
XLA Ops:
  0.0 0.1 maximum_bitcast_fusion.freq
  0.1 0.0 copy-start
  0.1 1.3 %copy-done = bf16[5120,128]{1,0:T(8,128)(2,1)S(1)} copy-done((bf16[5120,128]{1,0:T(8,128)(2,1)S(1)}, bf16[5120,128]{1,0:T(8,128)(2,1)}, u32[]{:S(2)}) %copy-start) | copy-done | bytes 1310744
  1.4 0.0 copy-start.1
  1.4 1.1 %copy-done.1 = bf16[64,5120]{1,0:T(8,128)(2,1)S(1)} copy-done((bf16[64,5120]{1,0:T(8,128)(2,1)S(1)}, bf16[64,5120]{1,0:T(8,128)(2,1)}, u32[]{:S(2)}) %copy-start.1) | copy-done | bytes 655384
  2.5 0.0 copy-start.2
  2.5 0.9 %copy-done.2 = bf16[5120,16]{0,1:T(8,128)(2,1)S(1)} copy-done((bf16[5120,16]{0,1:T(8,128)(2,1)S(1)}, bf16[5120,16]{0,1:T(8,128)(2,1)}, u32[]{:S(2)}) %copy-start.2) | copy-done | bytes 163864
  3.4 0.0 copy-start.3
  3.4 0.9 %copy-done.3 = bf16[5120,16]{0,1:T(8,128)(2,1)S(1)} copy-done((bf16[5120,16]{0,1:T(8,128)(2,1)S(1)}, bf16[5120,16]{0,1:T(8,128)(2,1)}, u32[]{:S(2)}) %copy-start.3) | copy-done | bytes 163864
  4.3 0.0 copy-start.4
  4.3 0.7 %copy-done.4 = f32[2,128]{1,0:T(2,128)S(1)} copy-done((f32[2,128]{1,0:T(2,128)S(1)}, f32[2,128]{1,0:T(2,128)}, u32[]{:S(2)}) %copy-start.4) | copy-done | bytes 1048
  5.0 0.0 copy-start.5
  5.0 0.7 %copy-done.5 = f32[1,128]{1,0:T(1,128)S(1)} copy-done((f32[1,128]{1,0:T(1,128)S(1)}, f32[1,128]{1,0:T(1,128)}, u32[]{:S(2)}) %copy-start.5) | copy-done | bytes 536
  5.7 58.5 %shard_map.64 = bf16[1024,128]{1,0:T(8,128)(2,1)S(1)} custom-call(bf16[64,5120]{1,0:T(8,128)(2,1)S(1)} %copy-done.1, bf16[5120,128]{1,0:T(8,128)(2,1)S(1)} %copy-done, bf16[16,5120]{1,0:T(8,128)(2,1)S(1)} %bitcast.4, bf16[16,5120]{1,0:T(8,128)(2,1)S(1)} %bitcast.5, f32[1,128]{1,0:T(1,128)S(1)} %copy-done.5, f32[2,128]{1,0:T(2,128)S(1)} %copy-done.4, ...), custom_call_target="tpu_custom_call" | custom-call | tf_op jit(solution)/shard_map/pallas_call | solution.py:428
  64.2 0.7 %copy.8 = bf16[1024,128]{1,0:T(8,128)(2,1)} copy(bf16[1024,128]{1,0:T(8,128)(2,1)S(1)} %shard_map.64) | data formatting | bytes 524288
  (1 shorter events, 0.0 us)
Async XLA Ops:
  0.1 1.3 %copy-start = (bf16[5120,128]{1,0:T(8,128)(2,1)S(1)}, bf16[5120,128]{1,0:T(8,128)(2,1)}, u32[]{:S(2)}) copy-start(bf16[5120,128]{1,0:T(8,128)(2,1)} %w_query.1) | copy-start | bytes 3932164
  1.4 1.1 %copy-start.1 = (bf16[64,5120]{1,0:T(8,128)(2,1)S(1)}, bf16[64,5120]{1,0:T(8,128)(2,1)}, u32[]{:S(2)}) copy-start(bf16[64,5120]{1,0:T(8,128)(2,1)} %tokens.1) | copy-start | bytes 1966084
  2.5 0.9 %copy-start.2 = (bf16[5120,16]{0,1:T(8,128)(2,1)S(1)}, bf16[5120,16]{0,1:T(8,128)(2,1)}, u32[]{:S(2)}) copy-start(bf16[5120,16]{0,1:T(8,128)(2,1)} %param.8) | copy-start | bytes 491524
  3.4 0.9 %copy-start.3 = (bf16[5120,16]{0,1:T(8,128)(2,1)S(1)}, bf16[5120,16]{0,1:T(8,128)(2,1)}, u32[]{:S(2)}) copy-start(bf16[5120,16]{0,1:T(8,128)(2,1)} %param.9) | copy-start | bytes 491524
  4.3 0.7 %copy-start.4 = (f32[2,128]{1,0:T(2,128)S(1)}, f32[2,128]{1,0:T(2,128)}, u32[]{:S(2)}) copy-start(f32[2,128]{1,0:T(2,128)} %k_gain.1) | copy-start | bytes 3076
  5.0 0.7 %copy-start.5 = (f32[1,128]{1,0:T(1,128)S(1)}, f32[1,128]{1,0:T(1,128)}, u32[]{:S(2)}) copy-start(f32[1,128]{1,0:T(1,128)} %q_gain.1) | copy-start | bytes 1540

commit v2 on v1

--- a/solution.py
+++ b/solution.py
@@ -99,8 +99,9 @@
 
 
 def layer_kernel(
-    tokens, w_query, w_kv_k, w_kv_v, q_gain, k_gain, freq, out,
-    tok, wq, wkv, q_stage, q_all, kv_all, cos_t, sin_t, acc_q, acc_kv,
+    tokens, w_query, w_kv_k, w_kv_v, q_gain_in, k_gain_in, freq_in, out,
+    q_gain, k_gain, freq,
+    tok, wq, wkv, q_stage, q_all, kv_all, cos_t, sin_t, acc_q, acc_kv, q_rot, k_rot, value, total,
     local_sem, right_send, left_send, tok_recv,
     core_send, core_recv, y_send, x_send, w_recv, diag_send, diag_recv,
     q_send, q_recv, kv_send, kv_recv,
@@ -141,6 +142,9 @@
         own(w_kv_v, wkv.at[1, s], 1),
         own(tokens, tok.at[z], 2),
         own(w_query, wq.at[:, pl.ds(0, head)], 3),
+        own(q_gain_in, q_gain, 4),
+        own(k_gain_in, k_gain, 5),
+        own(freq_in, freq, 6),
     ]
     for copy in locals_:
         copy.start()
@@ -265,6 +269,13 @@
     for i in range(last_piece + 1):
         diag_arrival(i, g).wait_recv()
         diag_arrival(i, 1 - g).wait_recv()
+    for i in range(last_piece + 1):
+        y_copy(i).wait_send()
+        x_copy(i, g).wait_send()
+        diag_copy(i, g).wait_send()
+        diag_copy(i, 1 - g).wait_send()
+    for copy in core_copies(False):
+        copy.wait_send()
 
     def result_copies(block):
         place = block * PLANE + s
@@ -347,69 +358,97 @@
             def _():
                 project(block, lambda chunk: None)
 
+    count = rows * PLANE * LINE
+    tile = rows * PLANE
+    lower = z < LINE // 2
+    last = jnp.where(lower, LINE - 1, 0)
+    factor = float(head) ** (-0.5) * 1.4426950408889634
+
+    def turn(values, gain, where):
+        scale = lax.rsqrt(jnp.mean(values * values, -1, keepdims=True) + EPS)
+        normed = values * scale * gain
+        return (normed * cos_t[where, :] + pltpu.roll(normed, head // 2, 1) * sin_t[where, :]).astype(jnp.bfloat16)
+
+    def take(block):
+        for copy in result_arrivals(block):
+            copy.wait_recv()
+        where = pl.ds(pl.multiple_of(block * tile, tile), tile)
+        places = pl.ds(block * PLANE, PLANE)
+        low_half = lax.broadcasted_iota(jnp.int32, (tile, head), 1) < head // 2
+        kv_0 = kv_all[0, places].reshape(tile, head).astype(jnp.float32)
+        kv_1 = kv_all[1, places].reshape(tile, head).astype(jnp.float32)
+        key = jnp.where(low_half, kv_0, pltpu.roll(kv_1, head // 2, 1))
+        val = jnp.where(low_half, pltpu.roll(kv_0, head // 2, 1), kv_1).astype(jnp.bfloat16)
+        value[where, :head] = val
+        value[where, head:] = jnp.ones_like(val)
+        query = q_all[places].reshape(tile, head).astype(jnp.float32)
+        q_rot[where, :] = turn(query, q_gain[...], where)
+        k_rot[where, :] = turn(key, k_gain[pl.ds(shared, 1), :], where)
+
+    def attend_part(first, stop, key_first, key_stop):
+        scores = lax.dot_general(
+            q_rot[first:stop, :], k_rot[key_first:key_stop, :], (((1,), (1,)), ((), ())),
+            preferred_element_type=jnp.float32,
+        )
+        weights = jnp.exp2(scores * factor)
+        if key_stop > first:
+            at_row = first + lax.broadcasted_iota(jnp.int32, scores.shape, 0)
+            at_col = key_first + lax.broadcasted_iota(jnp.int32, scores.shape, 1)
+            weights = jnp.where(at_col <= at_row, weights, 0.0)
+        return jnp.dot(
+            weights.astype(jnp.bfloat16), value[key_first:key_stop, :], preferred_element_type=jnp.float32
+        )
+
+    def store(first, stop, sums):
+        out[first:stop, :] = (sums[:, :head] / sums[:, head:]).astype(out.dtype)
+
+    @pl.loop(0, LINE - 1)
+    def _(i):
+        block = i + 1 - jnp.where(lower, 1, 0)
+        take(block)
+        for copy in result_copies(block):
+            copy.wait_send()
+
+    @pl.when(lower)
+    def _():
+        for i in range(LINE - 1):
+            store(i * tile, (i + 1) * tile, attend_part(i * tile, (i + 1) * tile, 0, (i + 1) * tile))
+
+    @pl.when(jnp.logical_not(lower))
+    def _():
+        for i in range(1, LINE):
+            total[i * tile : (i + 1) * tile, :] = attend_part(i * tile, (i + 1) * tile, tile, (i + 1) * tile)
+
+    for chunk in range(CHUNKS):
+        for block in range(LINE):
+
+            @pl.when(jnp.logical_and(block <= z, z < LINE - 1))
+            def _():
+                token_copy(block, chunk, True).wait_send()
+
+            @pl.when(jnp.logical_and(block >= z, z > 0))
+            def _():
+                token_copy(block, chunk, False).wait_send()
+
     @pl.when(jnp.logical_or(z == 0, z == LINE - 1))
     def _():
         project(LINE - 1 - z, lambda chunk: pass_on(3, chunk))
 
-    @pl.loop(0, LINE)
-    def _(block):
-        for copy in result_arrivals(block):
-            copy.wait_recv()
-
-    count = rows * PLANE * LINE
-    low_half = lax.broadcasted_iota(jnp.int32, (count, head), 1) < head // 2
-    kv_0 = kv_all[0].reshape(count, head).astype(jnp.float32)
-    kv_1 = kv_all[1].reshape(count, head).astype(jnp.float32)
-    key = jnp.where(low_half, kv_0, pltpu.roll(kv_1, head // 2, 1))
-    value = jnp.where(low_half, pltpu.roll(kv_0, head // 2, 1), kv_1).astype(jnp.bfloat16)
-    value = jnp.concatenate([value, jnp.ones_like(value)], 1)
-
-    def turn(values, gain, where):
-        scale = lax.rsqrt(jnp.mean(values * values, -1, keepdims=True) + EPS)
-        normed = values * scale * gain
-        return (normed * cos_t[where] + pltpu.roll(normed, head // 2, 1) * sin_t[where]).astype(jnp.bfloat16)
-
-    everything = slice(0, count)
-    query = q_all[...].reshape(count, head).astype(jnp.float32)
-    q_rot = turn(query, q_gain[...], everything)
-    k_rot = turn(key, k_gain[pl.ds(shared, 1), :], everything)
-    tile = rows * PLANE
-    factor = float(head) ** (-0.5) * 1.4426950408889634
-    for i in range(LINE):
-        scores = lax.dot_general(
-            q_rot[i * tile : (i + 1) * tile], k_rot[: (i + 1) * tile], (((1,), (1,)), ((), ())),
-            preferred_element_type=jnp.float32,
-        )
-        weights = jnp.exp2(scores * factor)
-        at_row = i * tile + lax.broadcasted_iota(jnp.int32, scores.shape, 0)
-        at_col = lax.broadcasted_iota(jnp.int32, scores.shape, 1)
-        weights = jnp.where(at_col <= at_row, weights, 0.0).astype(jnp.bfloat16)
-        total = jnp.dot(weights, value[: (i + 1) * tile], preferred_element_type=jnp.float32)
-        out[i * tile : (i + 1) * tile, :] = (total[:, :head] / total[:, head:]).astype(out.dtype)
-
-    for chunk in range(CHUNKS):
-        for block in range(LINE):
-
-            @pl.when(jnp.logical_and(block <= z, z < LINE - 1))
-            def _():
-                token_copy(block, chunk, True).wait_send()
-
-            @pl.when(jnp.logical_and(block >= z, z > 0))
-            def _():
-                token_copy(block, chunk, False).wait_send()
-
-    for i in range(last_piece + 1):
-        y_copy(i).wait_send()
-        x_copy(i, g).wait_send()
-        diag_copy(i, g).wait_send()
-        diag_copy(i, 1 - g).wait_send()
-    for copy in core_copies(False):
+    take(last)
+
+    @pl.when(lower)
+    def _():
+        store(count - tile, count, attend_part(count - tile, count, 0, count))
+
+    @pl.when(jnp.logical_not(lower))
+    def _():
+        store(0, tile, attend_part(0, tile, 0, tile))
+        for i in range(1, LINE):
+            first, stop = i * tile, (i + 1) * tile
+            store(first, stop, total[first:stop, :] + attend_part(first, stop, 0, tile))
+
+    for copy in result_copies(last):
         copy.wait_send()
-
-    @pl.loop(0, LINE)
-    def _(block):
-        for copy in result_copies(block):
-            copy.wait_send()
 
 
 def kernel_device(tokens, w_query, w_key, w_value, q_gain, k_gain):
@@ -422,15 +461,18 @@
     freq = jnp.concatenate([freq, freq])[None, :]
     bf16, f32 = jnp.bfloat16, jnp.float32
     dma = pltpu.SemaphoreType.DMA
-    hbm = pl.BlockSpec(memory_space=pl.ANY)
+    hbm = pl.BlockSpec(memory_space=pltpu.HBM)
     vmem = pl.BlockSpec(memory_space=pltpu.VMEM)
     blocks = LINE * PLANE
     return pl.pallas_call(
         layer_kernel,
         out_shape=jax.ShapeDtypeStruct((count, head), bf16),
-        in_specs=[hbm] * 4 + [vmem] * 3,
+        in_specs=[hbm] * 7,
         out_specs=vmem,
         scratch_shapes=[
+            pltpu.VMEM(q_gain.shape, f32),
+            pltpu.VMEM(k_gain.shape, f32),
+            pltpu.VMEM(freq.shape, f32),
             pltpu.VMEM((LINE, rows, width), bf16),
             pltpu.VMEM((width, PLANE * head), bf16),
             pltpu.VMEM((2, PLANE, thin, width), bf16),
@@ -441,7 +483,11 @@
             pltpu.VMEM((count, head), f32),
             pltpu.VMEM((rows, PLANE * head), f32),
             pltpu.VMEM((rows, 2 * PLANE * thin), f32),
-            dma((4,)),
+            pltpu.VMEM((count, head), bf16),
+            pltpu.VMEM((count, head), bf16),
+            pltpu.VMEM((count, 2 * head), bf16),
+            pltpu.VMEM((count, 2 * head), f32),
+            dma((7,)),
             dma((LINE, CHUNKS)),
             dma((LINE, CHUNKS)),
             dma((LINE, CHUNKS)),

time: 65.1 us -> 68.2 us (1.048)
  Pallas kernels: 58.5 us -> 61.6 us
    pallas_call x1, Pallas kernels: 58.5 us -> 61.6 us  [kernel_device(): pl.pallas_call(layer_kernel, out_shape=jax.ShapeDtypeStruct((count, head)...]
where the time goes in v2:
time: 68.2 us; the launch traced here: 67.9 us
  Pallas kernels  61.6 us (90%)
  local copies, waits for them, and re-layouts  6.28 us (9%)
    pallas_call x1, Pallas kernels, kernel_device(): pl.pallas_call(layer_kernel, out_shape=jax.ShapeDtypeStruct((count, head)...  61.6 us
    unnamed x13, local copies, waits for them, and re-layouts  6.28 us

profile of v2, /device:TPU:0, one launch (start us, length us, event | category | flops | bytes accessed | tf_op | source)
XLA Modules:
  0.0 67.9 jit_solution(18084029061559822542)
XLA Ops:
  0.0 0.1 maximum_bitcast_fusion.freq_in
  0.1 0.0 copy-start
  0.1 1.3 %copy-done = bf16[5120,128]{1,0:T(8,128)(2,1)S(1)} copy-done((bf16[5120,128]{1,0:T(8,128)(2,1)S(1)}, bf16[5120,128]{1,0:T(8,128)(2,1)}, u32[]{:S(2)}) %copy-start) | copy-done | bytes 1310744
  1.4 0.0 copy-start.1
  1.4 1.1 %copy-done.1 = bf16[64,5120]{1,0:T(8,128)(2,1)S(1)} copy-done((bf16[64,5120]{1,0:T(8,128)(2,1)S(1)}, bf16[64,5120]{1,0:T(8,128)(2,1)}, u32[]{:S(2)}) %copy-start.1) | copy-done | bytes 655384
  2.5 0.0 copy-start.2
  2.5 0.9 %copy-done.2 = bf16[5120,16]{0,1:T(8,128)(2,1)S(1)} copy-done((bf16[5120,16]{0,1:T(8,128)(2,1)S(1)}, bf16[5120,16]{0,1:T(8,128)(2,1)}, u32[]{:S(2)}) %copy-start.2) | copy-done | bytes 163864
  3.4 0.0 copy-start.3
  3.4 0.9 %copy-done.3 = bf16[5120,16]{0,1:T(8,128)(2,1)S(1)} copy-done((bf16[5120,16]{0,1:T(8,128)(2,1)S(1)}, bf16[5120,16]{0,1:T(8,128)(2,1)}, u32[]{:S(2)}) %copy-start.3) | copy-done | bytes 163864
  4.3 0.0 copy-start.4
  4.3 0.7 copy-done.4
  5.0 0.0 copy-start.5
  5.0 0.7 copy-done.5
  5.7 61.6 %shard_map.64 = bf16[1024,128]{1,0:T(8,128)(2,1)S(1)} custom-call(bf16[64,5120]{1,0:T(8,128)(2,1)S(1)} %copy-done.1, bf16[5120,128]{1,0:T(8,128)(2,1)S(1)} %copy-done, bf16[16,5120]{1,0:T(8,128)(2,1)S(1)} %bitcast.4, bf16[16,5120]{1,0:T(8,128)(2,1)S(1)} %bitcast.5, f32[1,128]{1,0:T(1,128)S(1)} %copy-done.5, f32[2,128]{1,0:T(2,128)S(1)} %copy-done.4, ...), custom_call_target="tpu_custom_call" | custom-call | tf_op jit(solution)/shard_map/pallas_call | solution.py:467
  67.2 0.7 %copy.8 = bf16[1024,128]{1,0:T(8,128)(2,1)} copy(bf16[1024,128]{1,0:T(8,128)(2,1)S(1)} %shard_map.64) | data formatting | bytes 524288
  (1 shorter events, 0.0 us)
Async XLA Ops:
  0.1 1.3 %copy-start = (bf16[5120,128]{1,0:T(8,128)(2,1)S(1)}, bf16[5120,128]{1,0:T(8,128)(2,1)}, u32[]{:S(2)}) copy-start(bf16[5120,128]{1,0:T(8,128)(2,1)} %w_query.1) | copy-start | bytes 3932164
  1.4 1.1 %copy-start.1 = (bf16[64,5120]{1,0:T(8,128)(2,1)S(1)}, bf16[64,5120]{1,0:T(8,128)(2,1)}, u32[]{:S(2)}) copy-start(bf16[64,5120]{1,0:T(8,128)(2,1)} %tokens.1) | copy-start | bytes 1966084
  2.5 0.9 %copy-start.2 = (bf16[5120,16]{0,1:T(8,128)(2,1)S(1)}, bf16[5120,16]{0,1:T(8,128)(2,1)}, u32[]{:S(2)}) copy-start(bf16[5120,16]{0,1:T(8,128)(2,1)} %param.8) | copy-start | bytes 491524
  3.4 0.9 %copy-start.3 = (bf16[5120,16]{0,1:T(8,128)(2,1)S(1)}, bf16[5120,16]{0,1:T(8,128)(2,1)}, u32[]{:S(2)}) copy-start(bf16[5120,16]{0,1:T(8,128)(2,1)} %param.9) | copy-start | bytes 491524
  4.3 0.7 copy-start.4
  5.0 0.7 copy-start.5

commit v3 on v2

--- a/solution.py
+++ b/solution.py
@@ -99,12 +99,12 @@
 
 
 def layer_kernel(
-    tokens, w_query, w_kv_k, w_kv_v, q_gain_in, k_gain_in, freq_in, out,
-    q_gain, k_gain, freq,
+    tokens, w_query, w_kv_k, w_kv_v, q_gain_in, k_gain_in, out,
+    q_gain, k_gain,
     tok, wq, wkv, q_stage, q_all, kv_all, cos_t, sin_t, acc_q, acc_kv, q_rot, k_rot, value, total,
     local_sem, right_send, left_send, tok_recv,
     core_send, core_recv, y_send, x_send, w_recv, diag_send, diag_recv,
-    q_send, q_recv, kv_send, kv_recv,
+    q_send, q_recv, kv_send, kv_recv, relay_send,
 ):
     me = lax.axis_index("row")
     g = lax.axis_index("groups")
@@ -144,7 +144,6 @@
         own(w_query, wq.at[:, pl.ds(0, head)], 3),
         own(q_gain_in, q_gain, 4),
         own(k_gain_in, k_gain, 5),
-        own(freq_in, freq, 6),
     ]
     for copy in locals_:
         copy.start()
@@ -226,7 +225,13 @@
         copy.start()
 
     spot = lax.broadcasted_iota(jnp.int32, cos_t.shape, 0).astype(jnp.float32)
-    angle = spot * freq[...]
+    pair = lax.broadcasted_iota(jnp.int32, (1, head), 1) % (head // 2)
+    coarse, fine = jnp.ones((1, head), jnp.float32), jnp.ones((1, head), jnp.float32)
+    for i in range(1, 8):
+        fine = jnp.where(pair % 8 == i, THETA ** (-2.0 * i / head), fine)
+    for i in range(1, head // 16):
+        coarse = jnp.where(pair // 8 == i, THETA ** (-16.0 * i / head), coarse)
+    angle = spot * (coarse * fine)
     lane = lax.broadcasted_iota(jnp.int32, cos_t.shape, 1)
     cos_t[...] = jnp.cos(angle)
     sine = jnp.sin(angle)
@@ -264,18 +269,15 @@
         if i > 0:
             take_x(i - 1)
     take_x(last_piece)
+    pass_on(2, 0)
     for copy in core_copies(True):
         copy.wait_recv()
+    pass_on(2, 1)
     for i in range(last_piece + 1):
         diag_arrival(i, g).wait_recv()
         diag_arrival(i, 1 - g).wait_recv()
-    for i in range(last_piece + 1):
-        y_copy(i).wait_send()
-        x_copy(i, g).wait_send()
-        diag_copy(i, g).wait_send()
-        diag_copy(i, 1 - g).wait_send()
-    for copy in core_copies(False):
-        copy.wait_send()
+    for chunk in range(2, CHUNKS - 1):
+        pass_on(2, chunk)
 
     def result_copies(block):
         place = block * PLANE + s
@@ -285,16 +287,49 @@
                 q_stage.at[block, t - 1], q_all.at[place], q_send.at[block, t - 1],
                 q_recv.at[block, t - 1], at(z, peers[t]),
             ))
-        for far in (0, 1):
-            for t in range(PLANE):
-                if far == 0 and t == 0:
-                    continue
-                i = far * PLANE + t - 1
-                copies.append(remote(
-                    kv_all.at[half, place], kv_all.at[half, place], kv_send.at[block, i],
-                    kv_recv.at[block, i], at(pair_z if far else z, peers[t]),
-                ))
+        for far, t in ((0, 1), (0, 2), (0, 3), (1, 0)):
+            i = far * PLANE + t - 1
+            copies.append(remote(
+                kv_all.at[half, place], kv_all.at[half, place], kv_send.at[block, i],
+                kv_recv.at[block, i], at(pair_z if far else z, peers[t]),
+            ))
         return copies
+
+    def wide_copies(block):
+        place = kv_all.at[half, block * PLANE + s]
+        return [
+            remote(place, place, kv_send.at[block, PLANE + t - 1], kv_recv.at[block, PLANE + t - 1], at(pair_z, peers[t]))
+            for t in (1, 2, 3)
+        ]
+
+    def relay_copies(block):
+        place = kv_all.at[1 - half, block * PLANE + s]
+        return [
+            remote(place, place, relay_send.at[block, t - 1], kv_recv.at[block, PLANE + t - 1], at(z, peers[t]))
+            for t in (1, 2, 3)
+        ]
+
+    def far_arrival(block):
+        place = kv_all.at[1 - half, block * PLANE + s]
+        return remote(place, place, kv_send.at[block, PLANE - 1], kv_recv.at[block, PLANE - 1], at(pair_z, s))
+
+    edge = jnp.logical_or(z == 0, z == LINE - 1)
+
+    def relay(block):
+        @pl.when(edge)
+        def _():
+            far_arrival(block).wait_recv()
+            for copy in relay_copies(block):
+                copy.start()
+
+    def wait_results(block):
+        for copy in result_copies(block):
+            copy.wait_send()
+
+        @pl.when(edge)
+        def _():
+            for copy in wide_copies(block) + relay_copies(block):
+                copy.wait_send()
 
     def result_arrivals(block):
         arrivals = []
@@ -304,9 +339,7 @@
                 place, place, q_send.at[block, t - 1], q_recv.at[block, t - 1], at(z, peers[t]),
             ))
         for far in (0, 1):
-            for t in range(PLANE):
-                if far == 0 and t == 0:
-                    continue
+            for t in (1, 2, 3):
                 i = far * PLANE + t - 1
                 place = kv_all.at[1 - half if far else half, block * PLANE + peers[t]]
                 arrivals.append(remote(
@@ -325,6 +358,11 @@
         for copy in result_copies(block):
             copy.start()
 
+        @pl.when(edge)
+        def _():
+            for copy in wide_copies(block):
+                copy.start()
+
     def products(block, cols):
         part_tok = tok[block, :, cols]
         q_part = jnp.dot(part_tok, wq[cols, :], preferred_element_type=jnp.float32)
@@ -346,8 +384,7 @@
         finish(block, acc_q[...], acc_kv[...])
 
     project(z, lambda chunk: None)
-    for chunk in range(CHUNKS):
-        pass_on(2, chunk)
+    pass_on(2, CHUNKS - 1)
     for distance in (1, 2):
 
         @pl.loop(0, 2)
@@ -357,6 +394,10 @@
             @pl.when(jnp.logical_and(block >= 0, block < LINE))
             def _():
                 project(block, lambda chunk: None)
+
+    @pl.when(jnp.logical_or(z == 0, z == LINE - 1))
+    def _():
+        project(LINE - 1 - z, lambda chunk: pass_on(3, chunk))
 
     count = rows * PLANE * LINE
     tile = rows * PLANE
@@ -372,6 +413,11 @@
     def take(block):
         for copy in result_arrivals(block):
             copy.wait_recv()
+
+        @pl.when(jnp.logical_not(edge))
+        def _():
+            far_arrival(block).wait_recv()
+
         where = pl.ds(pl.multiple_of(block * tile, tile), tile)
         places = pl.ds(block * PLANE, PLANE)
         low_half = lax.broadcasted_iota(jnp.int32, (tile, head), 1) < head // 2
@@ -402,12 +448,15 @@
     def store(first, stop, sums):
         out[first:stop, :] = (sums[:, :head] / sums[:, head:]).astype(out.dtype)
 
+    @pl.loop(0, LINE)
+    def _(block):
+        relay(block)
+
     @pl.loop(0, LINE - 1)
     def _(i):
         block = i + 1 - jnp.where(lower, 1, 0)
         take(block)
-        for copy in result_copies(block):
-            copy.wait_send()
+        wait_results(block)
 
     @pl.when(lower)
     def _():
@@ -419,6 +468,14 @@
         for i in range(1, LINE):
             total[i * tile : (i + 1) * tile, :] = attend_part(i * tile, (i + 1) * tile, tile, (i + 1) * tile)
 
+    for i in range(last_piece + 1):
+        y_copy(i).wait_send()
+        x_copy(i, g).wait_send()
+        diag_copy(i, g).wait_send()
+        diag_copy(i, 1 - g).wait_send()
+    for copy in core_copies(False):
+        copy.wait_send()
+
     for chunk in range(CHUNKS):
         for block in range(LINE):
 
@@ -429,10 +486,6 @@
             @pl.when(jnp.logical_and(block >= z, z > 0))
             def _():
                 token_copy(block, chunk, False).wait_send()
-
-    @pl.when(jnp.logical_or(z == 0, z == LINE - 1))
-    def _():
-        project(LINE - 1 - z, lambda chunk: pass_on(3, chunk))
 
     take(last)
 
@@ -447,8 +500,7 @@
             first, stop = i * tile, (i + 1) * tile
             store(first, stop, total[first:stop, :] + attend_part(first, stop, 0, tile))
 
-    for copy in result_copies(last):
-        copy.wait_send()
+    wait_results(last)
 
 
 def kernel_device(tokens, w_query, w_key, w_value, q_gain, k_gain):
@@ -456,9 +508,6 @@
     head = w_query.shape[1]
     thin = w_key.shape[1]
     count = rows * lax.axis_size("row")
-    half = head // 2
-    freq = THETA ** (-(jnp.arange(half, dtype=jnp.float32) * 2.0 / head))
-    freq = jnp.concatenate([freq, freq])[None, :]
     bf16, f32 = jnp.bfloat16, jnp.float32
     dma = pltpu.SemaphoreType.DMA
     hbm = pl.BlockSpec(memory_space=pltpu.HBM)
@@ -467,12 +516,11 @@
     return pl.pallas_call(
         layer_kernel,
         out_shape=jax.ShapeDtypeStruct((count, head), bf16),
-        in_specs=[hbm] * 7,
+        in_specs=[hbm] * 6,
         out_specs=vmem,
         scratch_shapes=[
             pltpu.VMEM(q_gain.shape, f32),
             pltpu.VMEM(k_gain.shape, f32),
-            pltpu.VMEM(freq.shape, f32),
             pltpu.VMEM((LINE, rows, width), bf16),
             pltpu.VMEM((width, PLANE * head), bf16),
             pltpu.VMEM((2, PLANE, thin, width), bf16),
@@ -487,7 +535,7 @@
             pltpu.VMEM((count, head), bf16),
             pltpu.VMEM((count, 2 * head), bf16),
             pltpu.VMEM((count, 2 * head), f32),
-            dma((7,)),
+            dma((6,)),
             dma((LINE, CHUNKS)),
             dma((LINE, CHUNKS)),
             dma((LINE, CHUNKS)),
@@ -502,11 +550,12 @@
             dma((LINE, 3)),
             dma((LINE, 7)),
             dma((LINE, 7)),
+            dma((LINE, 3)),
         ],
         compiler_params=pltpu.CompilerParams(
-            collective_id=0, has_side_effects=True, vmem_limit_bytes=48 * 1024 * 1024
+            collective_id=0, has_side_effects=True, vmem_limit_bytes=62 * 1024 * 1024
         ),
-    )(tokens, w_query, w_key.T, w_value.T, q_gain, k_gain, freq)
+    )(tokens, w_query, w_key.T, w_value.T, q_gain, k_gain)
 
 
 def per_device(*args):

time: 68.2 us -> 60 us (0.88)
  local copies, waits for them, and re-layouts: 6.28 us -> 1.67 us
  Pallas kernels: 61.6 us -> 58.1 us
    unnamed x13 -> x1, local copies, waits for them, and re-layouts: 6.28 us -> 1.67 us
    pallas_call x1, Pallas kernels: 61.6 us -> 58.1 us  [kernel_device(): pl.pallas_call(layer_kernel, out_shape=jax.ShapeDtypeStruct((count, head)...]
where the time goes in v3:
time: 60 us; the launch traced here: 59.8 us
  Pallas kernels  58.1 us (97%)
  local copies, waits for them, and re-layouts  1.67 us (3%)
    pallas_call x1, Pallas kernels, kernel_device(): pl.pallas_call(layer_kernel, out_shape=jax.ShapeDtypeStruct((count, head)...  58.1 us
    unnamed x1, local copies, waits for them, and re-layouts  1.67 us

profile of v3, /device:TPU:0, one launch (start us, length us, event | category | flops | bytes accessed | tf_op | source)
XLA Modules:
  0.0 59.8 jit_solution(13354247899826848135)
XLA Ops:
  0.0 58.1 %shard_map.64 = bf16[1024,128]{1,0:T(8,128)(2,1)} custom-call(bf16[64,5120]{1,0:T(8,128)(2,1)} %tokens.1, bf16[5120,128]{1,0:T(8,128)(2,1)} %w_query.1, bf16[16,5120]{1,0:T(8,128)(2,1)} %bitcast.2, bf16[16,5120]{1,0:T(8,128)(2,1)} %bitcast.3, f32[1,128]{1,0:T(1,128)} %q_gain_in.1, f32[2,128]{1,0:T(2,128)} %k_gain_in.1), custom_call_target="tpu_custom_call" | custom-call | tf_op jit(solution)/shard_map/pallas_call | solution.py:516
  58.1 1.7 %copy.8 = bf16[1024,128]{1,0:T(8,128)(2,1)} copy(bf16[1024,128]{1,0:T(8,128)(2,1)} %shard_map.64) | data formatting | bytes 524288
